TPU v7x, 32 devices: a whole 2x2x4 slice. The times are simulated.
32 devices in a mesh: inst: 8 (over z, x), tp: 4 (over y, core).
Axes of the slice: x: 2, y: 2, z: 4, core: 2. Of those that a mesh axis runs over, the one named last changes fastest.
Arguments:
- queries: bfloat16 [2, 256, 1024], P(None, 'inst', 'tp'), may hold values from -120 to 120
- stored_keys: bfloat16 [256, 128, 512], P('inst', None, 'tp'), may hold values from -6.1 to 6.1, as said below
- stored_values: bfloat16 [256, 128, 512], P('inst', None, 'tp'), may hold values from -6 to 6, as said below
- incoming_keys: bfloat16 [2, 256, 512], P(None, 'inst', 'tp'), may hold values from -6 to 6, as said below
- incoming_values: bfloat16 [2, 256, 512], P(None, 'inst', 'tp'), may hold values from -6 to 6, as said below
- cache_length_rows: int32 [256], P('inst'), may hold values from 2 to 128
- output_matrix: bfloat16 [1024, 4096], P('tp'), may hold values from -0.25 to 0.25
- adapter_down_weight: bfloat16 [32, 1024, 64], P('inst', 'tp'), may hold values from -0.1875 to 0.1875
- adapter_up_weight: bfloat16 [32, 64, 4096], P('inst', None, 'tp'), may hold values from -0.75 to 0.75
- host: int32 [256, 1], P('inst'), may hold values from 0 to 7; in each aligned block of 32 rows (0 to 31, 32 to 63, ...) at most 8 rows name the same one
- slot: int32 [256], P('inst'), may hold values from 0 to 3
Outputs:
- projected: bfloat16 [2, 256, 4096], P(None, 'inst', 'tp')
Inputs may be any that keep to these rules, and one draw needn't show every extreme that they name: In each instance's rows at most 8 rows name one host, a bound that some block reaches. `stored_keys`: copies c and c' of a head are equal where c // 4 == c' // 4. `incoming_keys`: copies equal as in stored_keys. `stored_values`: copies equal as in stored_keys. `incoming_values`: copies equal as in stored_keys.
All inputs are finite; a program needn't handle non-finite values.
Results may differ from a plain program's by a relative error of at most 0.02.
Values may be sent and summed in bfloat16 or wider, within the bound.
A program may use at most 64 MiB of HBM per device.

v0:
```python
import math

import jax
import jax.numpy as jnp
from jax import lax
from jax.sharding import PartitionSpec as P


def local_attention(query_rows, cached_keys, cached_values, fresh_keys, fresh_values, lengths):
    row_count = cached_keys.shape[0]
    slot_count = cached_keys.shape[1]
    head_width = cached_keys.shape[2]
    head_count = query_rows.shape[1] // head_width
    score_scale = 1.0 / math.sqrt(head_width)
    query_heads = query_rows.reshape(row_count, head_count, head_width)
    scores = (
        jnp.einsum("rhd,rcd->rhc", query_heads, cached_keys, preferred_element_type=jnp.float32)
        * score_scale
    )
    visible = jnp.arange(slot_count, dtype=jnp.int32)[None, None, :] < lengths[:, None, None]
    scores = jnp.where(visible, scores, -1e30)
    fresh_scores = (
        jnp.einsum("rhd,srd->rhs", query_heads, fresh_keys, preferred_element_type=jnp.float32)
        * score_scale
    )
    highest = jnp.maximum(
        jnp.max(scores, axis=-1, keepdims=True), jnp.max(fresh_scores, axis=-1, keepdims=True)
    )
    cached_exp = jnp.exp(scores - highest)
    fresh_exp = jnp.exp(fresh_scores - highest)
    denominator = jnp.sum(cached_exp, axis=-1, keepdims=True) + jnp.sum(
        fresh_exp, axis=-1, keepdims=True
    )
    cached_weight = (cached_exp / denominator).astype(jnp.bfloat16)
    fresh_weight = (fresh_exp / denominator).astype(jnp.bfloat16)
    mixed_heads = jnp.einsum(
        "rhc,rcd->rhd", cached_weight, cached_values, preferred_element_type=jnp.float32
    )
    mixed_heads = mixed_heads + jnp.einsum(
        "rhs,srd->rhd", fresh_weight, fresh_values, preferred_element_type=jnp.float32
    )
    return mixed_heads.astype(jnp.bfloat16).reshape(row_count, head_count * head_width)


def shards(
    queries,
    stored_keys,
    stored_values,
    incoming_keys,
    incoming_values,
    cache_length_rows,
    output_matrix,
    adapter_down_weight,
    adapter_up_weight,
    host,
    slot,
):
    step_count = queries.shape[0]
    row_count = queries.shape[1]
    resident_slots = adapter_down_weight.shape[0]
    column_total = adapter_up_weight.shape[2]
    attention_output = []
    for step_index in range(step_count):
        attention_output.append(
            local_attention(
                queries[step_index],
                stored_keys,
                stored_values,
                incoming_keys[: step_index + 1],
                incoming_values[: step_index + 1],
                cache_length_rows,
            )
        )
    features = jnp.concatenate(attention_output, axis=0)
    base_terms = jnp.dot(features, output_matrix, preferred_element_type=jnp.float32)
    base_sum = lax.psum_scatter(
        base_terms.astype(jnp.bfloat16), "tp", scatter_dimension=1, tiled=True
    ).astype(jnp.float32)
    destination = jnp.tile(host[:, 0], step_count)
    slot_all = jnp.tile(slot, step_count)
    adapter_all = destination * resident_slots + slot_all
    partition_piece = lax.all_gather(adapter_down_weight, "inst", axis=0, tiled=True)
    piece_count = partition_piece.shape[0]
    selector = (adapter_all[:, None] == jnp.arange(piece_count, dtype=jnp.int32)[None, :]).astype(
        jnp.float32
    )
    projected = jnp.einsum(
        "rf,afk->rak", features, partition_piece, preferred_element_type=jnp.float32
    )
    partial_value = jnp.sum(selector[:, :, None] * projected, axis=1)
    summed = lax.psum(partial_value, "tp").astype(jnp.bfloat16)
    partition_piece = lax.all_gather(adapter_up_weight, "inst", axis=0, tiled=True)
    piece_count = partition_piece.shape[0]
    selector = (adapter_all[:, None] == jnp.arange(piece_count, dtype=jnp.int32)[None, :]).astype(
        jnp.float32
    )
    expanded = jnp.einsum(
        "rk,akc->rac", summed, partition_piece, preferred_element_type=jnp.float32
    )
    adapter_update = jnp.sum(selector[:, :, None] * expanded, axis=1)
    projected = (base_sum + adapter_update).astype(jnp.bfloat16)
    return projected.reshape(step_count, row_count, column_total)


def solution(mesh):
    return jax.shard_map(
        shards,
        mesh=mesh,
        in_specs=(
            P(None, "inst", "tp"),
            P("inst", None, "tp"),
            P("inst", None, "tp"),
            P(None, "inst", "tp"),
            P(None, "inst", "tp"),
            P("inst"),
            P("tp", None),
            P("inst", "tp", None),
            P("inst", None, "tp"),
            P("inst", None),
            P("inst"),
        ),
        out_specs=P(None, "inst", "tp"),
        check_vma=False,
    )
```

profile of v0, /device:TPU:0, one launch (start us, length us, event | category | flops | bytes accessed | tf_op | source)
XLA Modules:
  0.0 140.0 jit_solution(11398292143659507601)
XLA Ops:
  7.4 0.0 copy-start
  7.4 0.0 copy-start.1
  7.4 0.0 copy-start.2
  7.4 0.0 all-gather.3.cloned.1.call-start
  7.4 0.7 all-gather.3.cloned.1.call-update
  8.1 0.0 all-gather.5.cloned.1.call-start
  8.1 0.7 all-gather.5.cloned.1.call-update
  8.8 0.0 reduce-scatter.2.cloned.1.call-start
  8.9 0.7 fusion.25
  9.7 0.7 iota_compare_fusion.1
  10.4 0.9 fusion.28
  11.3 1.9 %fusion.27 = (f32[32,2]{1,0:T(8,128)S(1)}, f32[32,2,128]{2,1,0:T(2,128)S(1)}) fusion(bf16[32,2,128]{2,1,0:T(2,128)(2,1)S(1)} %reshape_squeeze.7, bf16[32,128,128]{2,1,0:T(8,128)(2,1)} %param.12, pred[32,128]{1,0:T(8,128)(4,1)S(1)} %iota_compare_fusion.1), kind=kOutput, calls=%fused_computation.52 | convolution fusion | flops 2121664 | bytes 1102080 | tf_op jit(solution)/shard_map/rhd,rcd->rhc/dot_general | solution.py:17
  13.2 0.0 copy-start.3
  13.2 0.0 copy-start.4
  13.3 0.1 fusion.8
  13.3 0.2 fusion.7
  13.5 0.7 slice_bitcast_fusion
  14.2 0.2 fusion.21
  14.4 2.0 %fusion.26 = (f32[32,2]{1,0:T(8,128)S(1)}, f32[32,2,128]{2,1,0:T(2,128)S(1)}) fusion(bf16[32,2,128]{2,1,0:T(2,128)(2,1)S(1)} %reshape_squeeze.6, bf16[32,128,128]{2,1,0:T(8,128)(2,1)} %param.12, pred[32,128]{1,0:T(8,128)(4,1)S(1)} %iota_compare_fusion.1), kind=kOutput, calls=%fused_computation.51 | convolution fusion | flops 2121664 | bytes 1102080 | tf_op jit(solution)/shard_map/rhd,rcd->rhc/dot_general | solution.py:17
  16.4 0.2 fusion.6
  16.6 0.7 bitcast_convert_fusion
  17.3 1.7 %fusion.3 = bf16[32,2,128]{2,1,0:T(2,128)(2,1)S(1)} fusion(bf16[32,128,128]{2,1,0:T(8,128)(2,1)} %param.13, f32[32,2,128]{2,1,0:T(2,128)S(1)} %get-tuple-element.10, f32[32,128]{1,0:T(8,128)S(1)} %bitcast_convert_fusion, f32[32,2]{1,0:T(8,128)S(1)} %get-tuple-element.6, f32[32,2]{1,0:T(8,128)S(1)} %get-tuple-element.5, f32[32,2]{1,0:T(8,128)S(1)} %multiply_maximum_fusion), kind=kOutput, calls=%fused_computation.11 | convolution fusion | flops 2146304 | bytes 1114880 | tf_op jit(solution)/shard_map/rhc,rcd->rhd/dot_general | solution.py:36
  19.0 0.0 copy-done.2
  19.0 0.4 fusion.9
  19.4 0.0 copy-done.1
  19.4 0.3 fusion.4
  19.7 0.0 copy-done
  19.7 1.3 convolution_convert_fusion
  21.0 0.0 reduce-scatter.2.cloned.1.call-update
  21.0 0.0 copy-done.3
  21.0 0.0 copy-done.4
  21.0 0.1 add.43
  21.1 32.1 %all-gather.3.cloned.1.call-done = bf16[32,256,64]{1,2,0:T(8,128)(2,1)} async-done(((bf16[4,256,64]{1,2,0:T(8,128)(2,1)}), bf16[32,256,64]{1,2,0:T(8,128)(2,1)}) %all-gather.3.cloned.1.call-update) | async-done | bytes 1048592 | tf_op jit(solution)/shard_map/all_gather | solution.py:82
  53.2 1.9 %fusion = f32[64,64]{1,0:T(8,128)S(1)} fusion(bf16[32,256,64]{1,2,0:T(8,128)(2,1)} %all-gather.3.cloned.1.call-done, f32[64,32]{0,1:T(8,128)S(1)} %fusion.18, bf16[64,256]{1,0:T(8,128)(2,1)S(1)} %bitcast_dynamic-update-slice_fusion), kind=kOutput, calls=%fused_computation.3 | convolution fusion | flops 67366912 | bytes 1105920 | tf_op jit(solution)/shard_map/rf,afk->rak/dot_general | solution.py:87
  55.1 10.3 %psum.7 = bf16[64,64]{1,0:T(8,128)(2,1)S(1)} all-reduce(f32[64,64]{1,0:T(8,128)S(1)} %fusion), channel_id=1, replica_groups=mesh['inst'=8,'tp'=4] {'tp'}, use_global_device_ids=true, to_apply=%region_8.9 | all-reduce | flops 4096 | bytes 24576 | tf_op jit(solution)/shard_map/psum | solution.py:91
  65.3 62.2 %all-gather.5.cloned.1.call-done = bf16[32,64,1024]{2,1,0:T(8,128)(2,1)} async-done(((bf16[4,64,1024]{2,1,0:T(8,128)(2,1)}), bf16[32,64,1024]{2,1,0:T(8,128)(2,1)}) %all-gather.5.cloned.1.call-update) | async-done | bytes 4194320 | tf_op jit(solution)/shard_map/all_gather | solution.py:92
  127.5 3.4 %multiply_reduce_fusion = f32[64,1024]{1,0:T(8,128)S(1)} fusion(f32[64,32]{0,1:T(8,128)S(1)} %fusion.18, bf16[32,64,1024]{2,1,0:T(8,128)(2,1)} %all-gather.5.cloned.1.call-done, bf16[64,64]{1,0:T(8,128)(2,1)S(1)} %psum.7), kind=kOutput, calls=%fused_computation | convolution fusion | flops 272564224 | bytes 4472832 | tf_op jit(solution)/shard_map/rk,akc->rac/dot_general | solution.py:97
  131.0 0.0 reduce-scatter.2.cloned.1.call-done
  131.0 1.6 %add_convert_fusion = bf16[64,1024]{1,0:T(8,128)(2,1)} fusion(f32[64,1024]{1,0:T(8,128)S(1)} %multiply_reduce_fusion, bf16[64,1024]{1,0:T(8,128)(2,1)} %reduce-scatter.2.cloned.1.call-done), kind=kLoop, calls=%fused_computation.13 | loop fusion | flops 196608 | bytes 524288 | tf_op jit(solution)/shard_map/convert_element_type | solution.py:101
  (11 shorter events, 0.1 us)
Async XLA Ops:
  7.4 12.3 %copy-start = (bf16[256,4096]{1,0:T(8,128)(2,1)S(1)}, bf16[256,4096]{1,0:T(8,128)(2,1)}, u32[]{:S(2)}) copy-start(bf16[256,4096]{1,0:T(8,128)(2,1)} %param.17) | copy-start | bytes 6291460
  7.4 12.0 %copy-start.1 = (bf16[2,32,128]{2,1,0:T(8,128)(2,1)S(1)}, bf16[2,32,128]{2,1,0:T(8,128)(2,1)}, u32[]{:S(2)}) copy-start(bf16[2,32,128]{2,1,0:T(8,128)(2,1)} %param.15) | copy-start | bytes 49156
  7.4 11.6 %copy-start.2 = (bf16[32,128,128]{2,1,0:T(8,128)(2,1)S(1)}, bf16[32,128,128]{2,1,0:T(8,128)(2,1)}, u32[]{:S(2)}) copy-start(bf16[32,128,128]{2,1,0:T(8,128)(2,1)} %param.13) | copy-start | bytes 3145732
  7.4 45.8 %all-gather.3.cloned.1.call-start = ((), (), s32[]{:S(2)}) async-start(), calls=%async_computation.2 | async-start | bytes 1179648 | tf_op jit(solution)/shard_map/all_gather | solution.py:82
  8.1 119.4 %all-gather.5.cloned.1.call-start = ((), (), s32[]{:S(2)}) async-start(), calls=%async_computation.3 | async-start | bytes 4718592 | tf_op jit(solution)/shard_map/all_gather | solution.py:92
  8.8 122.2 %reduce-scatter.2.cloned.1.call-start = ((), (), s32[]{:S(2)}) async-start(), calls=%async_computation.1 | async-start | bytes 655360 | tf_op jit(solution)/shard_map/reduce_scatter | solution.py:76
  13.2 7.8 %copy-start.3 = (s32[32]{0:T(128)S(1)}, s32[32]{0:T(128)}, u32[]{:S(2)}) copy-start(s32[32]{0:T(128)} %param.21) | copy-start | bytes 388
  13.2 7.8 %copy-start.4 = (s32[32,1]{0,1:T(1,128)S(1)}, s32[32,1]{0,1:T(1,128)}, u32[]{:S(2)}) copy-start(s32[32,1]{0,1:T(1,128)} %param.20) | copy-start | bytes 388
Sparse Core Ops, SparseCore 0:
  10.3 42.8 all-gather.2
  55.3 72.1 all-gather.4
Sparse Core Ops, SparseCore 1:
  21.1 24.3 reduce-scatter.1
where the time goes:
time: 141 us; the launch traced here: 140 us
  waiting for transfers between devices  95.7 us (68%)
  between operations  15 us (11%)
  matrix products  13.9 us (10%)
  blocking collectives  10.3 us (7%)
  other arithmetic  3.51 us (2%)
  local copies, waits for them, and re-layouts  1.58 us (1%)
    all_gather x1, waiting for transfers between devices, shards(): lax.all_gather(adapter_up_weight, 'inst', axis=0, tiled=True)  62.2 us
    all_gather x1, waiting for transfers between devices, shards(): lax.all_gather(adapter_down_weight, 'inst', axis=0, tiled=True)  32.1 us
    psum x1, blocking collectives, shards(): summed = lax.psum(partial_value, 'tp').astype(jnp.bfloat16)  10.3 us
    dot_general x2, matrix products, local_attention(): jnp.einsum('rhd,rcd->rhc', query_heads, cached_keys, preferred_element_ty...  3.91 us
    dot_general x1, matrix products, shards(): jnp.einsum('rk,akc->rac', summed, partition_piece, preferred_element_type...  3.44 us
  transfers between devices with their start and end apart: 3, of which 2 were waited for; matrix products, arithmetic and copies ran while one was open for 12% of the time, Pallas kernels for 0%

commit v1 on v0

v1 whole, which is shorter than its diff:
```python
import functools
import math

import jax
import jax.numpy as jnp
from jax import lax
from jax.experimental import pallas as pl
from jax.experimental.pallas import tpu as pltpu
from jax.sharding import PartitionSpec as P

MESH = pl.DeviceIdType.MESH
BF = jnp.bfloat16
F32 = jnp.float32
TILE = 16
LANES = 128


def log2(n):
    assert n & (n - 1) == 0
    return n.bit_length() - 1


def rows_iota(shape):
    return lax.broadcasted_iota(jnp.int32, shape, 0)


def lanes_iota(shape):
    return lax.broadcasted_iota(jnp.int32, shape, 1)


def dot(a, b):
    return jnp.dot(a, b, preferred_element_type=F32)


def dot_t(a, b):
    return lax.dot_general(a, b, (((1,), (1,)), ((), ())), preferred_element_type=F32)


def one_hot(mask):
    return jnp.where(mask, 1.0, 0.0).astype(BF)


def kernel(
    n_inst, n_tp, cap,
    q_ref, kn_ref, vn_ref, len_ref, host_ref, slot_ref,
    k_hbm, v_hbm, w_hbm, dn_hbm, up_hbm,
    out_ref,
    k_buf, v_buf, w_buf, dn_buf, up_buf, dn_flat,
    meta_s, meta_r, x_s, x_r, dl_s, dl_r, rk_s, rk_r,
    b1_s, b1_r, b2_s, b2_r, own,
    in_sem, meta_ss, meta_rs, x_ss, x_rs, dl_ss, dl_rs, rk_ss, rk_rs,
    b1_ss, b1_rs, b2_ss, b2_rs,
):
    steps, rows, width = q_ref.shape
    head = kn_ref.shape[2]
    heads = width // head
    slots = k_buf.shape[1]
    per_row = steps * heads
    cols = rows * per_row
    pack = meta_s.shape[1]
    total = n_inst * pack
    adapters, _, rank = dn_buf.shape
    chunks = adapters * rank // LANES
    out_cols = up_buf.shape[2]
    n_y = n_tp // 2
    me = lax.axis_index("inst")
    tp = lax.axis_index("tp")
    y = tp // 2
    core = lax.rem(tp, 2)

    def inst_at(k):
        return (lax.rem(me + k + n_inst, n_inst), tp)

    def tp_at(k):
        return (me, lax.rem(tp + k, n_tp))

    def remote(src, dst, send, recv, where):
        return pltpu.make_async_remote_copy(
            src_ref=src, dst_ref=dst, send_sem=send, recv_sem=recv,
            device_id=where, device_id_type=MESH,
        )

    barrier = pltpu.get_barrier_semaphore()
    for k in range(1, n_inst):
        pl.semaphore_signal(barrier, inc=1, device_id=inst_at(k), device_id_type=MESH)
    for k in range(1, n_tp):
        pl.semaphore_signal(barrier, inc=1, device_id=tp_at(k), device_id_type=MESH)
    loads = []
    for at, (src, dst) in enumerate(
        ((k_hbm, k_buf), (v_hbm, v_buf), (w_hbm, w_buf), (dn_hbm, dn_buf), (up_hbm, up_buf))
    ):
        load = pltpu.make_async_copy(src, dst, in_sem.at[at])
        load.start()
        loads.append(load)

    host_lane = host_ref[...].astype(F32)
    slot_lane = slot_ref[...].astype(F32)
    here = me.astype(F32)
    square = (rows, rows)
    ri, li = rows_iota(square), lanes_iota(square)
    host_col = jnp.sum(jnp.where(ri == li, host_lane, 0.0), axis=1, keepdims=True)
    same = jnp.broadcast_to(host_col, square) == jnp.broadcast_to(host_lane, square)
    pos_lane = jnp.sum(jnp.where(same & (ri < li), 1.0, 0.0), axis=0, keepdims=True)
    pos_col = jnp.sum(jnp.where(same & (li < ri), 1.0, 0.0), axis=1, keepdims=True)

    def place(host, pos):
        away = host - here
        away = jnp.where(away < 0.0, away + float(n_inst), away)
        return away * float(pack) + pos

    to_lane = place(host_lane, pos_lane).astype(jnp.int32)
    to_col = place(host_col, pos_col).astype(jnp.int32)
    pack_i = rows_iota((total, rows))
    packs = [pack_i == to_lane + step * cap for step in range(steps)]
    slot_packed = jnp.zeros((total, 1), F32)
    for chosen in packs:
        slot_packed += jnp.sum(jnp.where(chosen, slot_lane, 0.0), axis=1, keepdims=True)
    slot_packed = jnp.broadcast_to(slot_packed, (total, LANES)).astype(BF)
    meta_s[...] = slot_packed.reshape(n_inst, pack, LANES)
    meta_r[0] = slot_packed[:pack]

    pl.semaphore_wait(barrier, n_inst - 1 + n_tp - 1)
    meta_copies = []
    for k in range(1, n_inst):
        copy = remote(meta_s.at[k], meta_r.at[k], meta_ss.at[k], meta_rs.at[k], inst_at(k))
        copy.start()
        meta_copies.append(copy)

    ci = rows_iota((cols, cols))
    cj = lanes_iota((cols, cols))
    into = one_hot(cj == ((ci & (per_row - 1)) << log2(rows)) + (ci >> log2(per_row)))
    back = one_hot(ci == ((cj & (per_row - 1)) << log2(rows)) + (cj >> log2(per_row)))
    q_all = jnp.concatenate(
        [q_ref[s, :, h * head:(h + 1) * head] for s in range(steps) for h in range(heads)], axis=0
    )
    q_lines = dot(into, q_all)
    q_bf = q_lines.astype(BF)
    spread = rows_iota((cols, rows)) >> log2(per_row) == lanes_iota((cols, rows))
    lengths = jnp.sum(
        jnp.where(spread, len_ref[...].astype(F32), 0.0), axis=1, keepdims=True
    ).astype(jnp.int32)
    spread_bf = one_hot(spread)
    scale = 1.0 / math.sqrt(head)
    step_of = (rows_iota((cols, 1)) & (per_row - 1)) >> log2(heads)
    fresh = []
    for s in range(steps):
        value = jnp.sum(q_lines * dot(spread_bf, kn_ref[s]), axis=1, keepdims=True) * scale
        fresh.append(jnp.where(step_of >= s, value, -1e30))
    group = TILE // per_row
    group_of = rows_iota((TILE, slots)) >> log2(per_row)
    loads[0].wait()
    scores = []
    for g in range(rows // group):
        keys = k_buf[g * group:(g + 1) * group].reshape(group * slots, head)
        raw = dot_t(q_bf[g * TILE:(g + 1) * TILE], keys)
        picked = raw[:, :slots]
        for j in range(1, group):
            picked = jnp.where(group_of == j, raw[:, j * slots:(j + 1) * slots], picked)
        scores.append(picked)
    scores = jnp.concatenate(scores, axis=0) * scale
    scores = jnp.where(lanes_iota((cols, slots)) < lengths, scores, -1e30)
    highest = jnp.max(scores, axis=1, keepdims=True)
    for value in fresh:
        highest = jnp.maximum(highest, value)
    cached_exp = jnp.exp(scores - highest)
    fresh_exp = [jnp.exp(value - highest) for value in fresh]
    denominator = jnp.sum(cached_exp, axis=1, keepdims=True)
    for value in fresh_exp:
        denominator += value
    weights = cached_exp / denominator
    mixed = jnp.zeros((cols, head), F32)
    for s in range(steps):
        share = (fresh_exp[s] / denominator).astype(BF).astype(F32)
        mixed += share * dot(spread_bf, vn_ref[s])
    loads[1].wait()
    parts = []
    for g in range(rows // group):
        values = v_buf[g * group:(g + 1) * group].reshape(group * slots, head)
        own_w = weights[g * TILE:(g + 1) * TILE]
        blocked = jnp.concatenate(
            [jnp.where(group_of == j, own_w, 0.0) for j in range(group)], axis=1
        ).astype(BF)
        parts.append(dot(blocked, values))
    mixed = (mixed + jnp.concatenate(parts, axis=0)).astype(BF)
    lines = dot(back, mixed).astype(BF)
    features = []
    for s in range(steps):
        at = s * heads * rows
        features.append(jnp.concatenate(
            [lines[at + h * rows:at + (h + 1) * rows] for h in range(heads)], axis=1
        ))

    packed = dot(one_hot(packs[0]), features[0])
    for s in range(1, steps):
        packed += dot(one_hot(packs[s]), features[s])
    packed = packed.astype(BF)
    x_s[...] = packed.reshape(n_inst, pack, width)
    x_copies = []
    for k in range(1, n_inst):
        copy = remote(x_s.at[k], x_r.at[k], x_ss.at[k], x_rs.at[k], inst_at(k))
        copy.start()
        x_copies.append(copy)
    x_r[0] = packed[:pack]

    feats = jnp.concatenate(features, axis=0)
    loads[2].wait()

    def base_part(ky, parity):
        at = (lax.rem(y + ky, n_y) * 2 + parity) * out_cols
        return dot(feats, w_buf[:, pl.ds(pl.multiple_of(at, out_cols), out_cols)])

    b1_copies = {}
    for ky in reversed(range(n_y)):
        b1_s[ky] = base_part(ky, 1 - core).astype(BF)
        copy = remote(
            b1_s.at[ky], b1_r.at[ky], b1_ss.at[ky], b1_rs.at[ky], (me, y * 2 + 1 - core)
        )
        copy.start()
        b1_copies[ky] = copy
    for ky in reversed(range(n_y)):
        own[ky] = base_part(ky, core)

    loads[3].wait()
    flat = jnp.zeros((dn_buf.shape[1], adapters * rank), F32)
    tr, tl = rows_iota((rank, adapters * rank)), lanes_iota((rank, adapters * rank))
    for a in range(adapters):
        flat += dot(dn_buf[a], one_hot(tl == tr + a * rank))
    dn_flat[...] = flat.astype(BF)
    for copy in meta_copies:
        copy.wait_recv()
    slot_got = meta_r[...].reshape(total, LANES).astype(F32)
    lane = lanes_iota((total, LANES))
    masks = [
        slot_got == ((lane + c * LANES) >> log2(rank)).astype(F32) for c in range(chunks)
    ]
    for copy in x_copies:
        copy.wait_recv()
    ranked = dot(x_r[...].reshape(total, width), dn_flat[...])
    folded = jnp.zeros((total, LANES), F32)
    for c in range(chunks):
        folded += jnp.where(masks[c], ranked[:, c * LANES:(c + 1) * LANES], 0.0)
    rk_s[...] = folded.astype(BF)
    rk_copies = []
    for k in range(1, n_tp):
        copy = remote(rk_s, rk_r.at[k], rk_ss.at[k], rk_rs.at[k], tp_at(k))
        copy.start()
        rk_copies.append(copy)

    b2_copies = []
    for ky in range(1, n_y):
        b1_copies[ky].wait_recv()
        b2_s[ky] = (own[ky] + b1_r[ky].astype(F32)).astype(BF)
        copy = remote(
            b2_s.at[ky], b2_r.at[ky], b2_ss.at[ky], b2_rs.at[ky],
            (me, lax.rem(y + ky, n_y) * 2 + core),
        )
        copy.start()
        b2_copies.append(copy)

    loads[4].wait()
    for k, copy in enumerate(rk_copies, 1):
        copy.wait_recv()
        folded += rk_r[k].astype(F32)
    wide = jnp.concatenate(
        [jnp.where(masks[c], folded, 0.0) for c in range(chunks)], axis=1
    ).astype(BF)
    delta = dot(wide, up_buf[...].reshape(adapters * rank, out_cols)).astype(BF)
    dl_s[...] = delta.reshape(n_inst, pack, out_cols)
    dl_copies = []
    for k in range(1, n_inst):
        copy = remote(dl_s.at[k], dl_r.at[k], dl_ss.at[k], dl_rs.at[k], inst_at(-k))
        copy.start()
        dl_copies.append(copy)
    dl_r[0] = delta[:pack]

    b1_copies[0].wait_recv()
    base = own[0] + b1_r[0].astype(F32)
    for ky, copy in enumerate(b2_copies, 1):
        copy.wait_recv()
        base += b2_r[ky].astype(F32)
    own[0] = base
    unpack = jnp.concatenate(
        [one_hot(lanes_iota((rows, total)) == to_col + step * cap) for step in range(steps)], axis=0
    )
    for copy in dl_copies:
        copy.wait_recv()
    result = own[0] + dot(unpack, dl_r[...].reshape(total, out_cols))
    out_ref[...] = result.astype(BF).reshape(steps, rows, out_cols)

    for copy in meta_copies + x_copies + rk_copies + b2_copies + dl_copies:
        copy.wait_send()
    for ky in range(n_y):
        b1_copies[ky].wait_send()


def shards(
    n_inst, n_tp,
    queries, stored_keys, stored_values, incoming_keys, incoming_values, cache_length_rows,
    output_matrix, adapter_down_weight, adapter_up_weight, host, slot,
):
    steps, rows, width = queries.shape
    adapters, _, rank = adapter_down_weight.shape
    out_cols = adapter_up_weight.shape[2]
    cap = max(1, 2 * rows // n_inst)
    pack = -(-steps * cap // TILE) * TILE
    total = n_inst * pack
    n_y = n_tp // 2
    lines = steps * rows
    vmem = pl.BlockSpec(memory_space=pltpu.VMEM)
    far = pl.BlockSpec(memory_space=pl.ANY)
    sem = pltpu.SemaphoreType.DMA
    return pl.pallas_call(
        functools.partial(kernel, n_inst, n_tp, cap),
        out_shape=jax.ShapeDtypeStruct((steps, rows, out_cols), BF),
        in_specs=[vmem] * 6 + [far] * 5,
        out_specs=vmem,
        scratch_shapes=[
            pltpu.VMEM(stored_keys.shape, BF),
            pltpu.VMEM(stored_values.shape, BF),
            pltpu.VMEM(output_matrix.shape, BF),
            pltpu.VMEM(adapter_down_weight.shape, BF),
            pltpu.VMEM(adapter_up_weight.shape, BF),
            pltpu.VMEM((width, adapters * rank), BF),
            pltpu.VMEM((n_inst, pack, LANES), BF),
            pltpu.VMEM((n_inst, pack, LANES), BF),
            pltpu.VMEM((n_inst, pack, width), BF),
            pltpu.VMEM((n_inst, pack, width), BF),
            pltpu.VMEM((n_inst, pack, out_cols), BF),
            pltpu.VMEM((n_inst, pack, out_cols), BF),
            pltpu.VMEM((total, LANES), BF),
            pltpu.VMEM((n_tp, total, LANES), BF),
            pltpu.VMEM((n_y, lines, out_cols), BF),
            pltpu.VMEM((n_y, lines, out_cols), BF),
            pltpu.VMEM((n_y, lines, out_cols), BF),
            pltpu.VMEM((n_y, lines, out_cols), BF),
            pltpu.VMEM((n_y, lines, out_cols), F32),
            sem((5,)),
            sem((n_inst,)), sem((n_inst,)),
            sem((n_inst,)), sem((n_inst,)),
            sem((n_inst,)), sem((n_inst,)),
            sem((n_tp,)), sem((n_tp,)),
            sem((n_y,)), sem((n_y,)),
            sem((n_y,)), sem((n_y,)),
        ],
        compiler_params=pltpu.CompilerParams(
            collective_id=0, has_side_effects=True, vmem_limit_bytes=48 * 1024 * 1024
        ),
    )(
        queries, incoming_keys, incoming_values,
        cache_length_rows.reshape(1, rows), host.reshape(1, rows), slot.reshape(1, rows),
        stored_keys, stored_values, output_matrix, adapter_down_weight, adapter_up_weight,
    )


def solution(mesh):
    return jax.shard_map(
        functools.partial(shards, mesh.shape["inst"], mesh.shape["tp"]),
        mesh=mesh,
        in_specs=(
            P(None, "inst", "tp"),
            P("inst", None, "tp"),
            P("inst", None, "tp"),
            P(None, "inst", "tp"),
            P(None, "inst", "tp"),
            P("inst"),
            P("tp", None),
            P("inst", "tp", None),
            P("inst", None, "tp"),
            P("inst", None),
            P("inst"),
        ),
        out_specs=P(None, "inst", "tp"),
        check_vma=False,
    )
```

time: 141 us -> 36 us (0.26)
  waiting for transfers between devices: 95.7 us -> 0 us
  Pallas kernels: 0 us -> 24.5 us
  between operations: 15 us -> 0.03 us
  matrix products: 13.9 us -> 0 us
  blocking collectives: 10.3 us -> 0 us
  local copies, waits for them, and re-layouts: 1.58 us -> 11 us
  other arithmetic: 3.51 us -> 0 us
    all_gather x2 -> x0, waiting for transfers between devices: 94.3 us -> none  [the longest x1 62.2 us: shards(): lax.all_gather(adapter_up_weight, 'inst', axis=0, tiled=True)]
    pallas_call x0 -> x1, Pallas kernels: none -> 24.5 us  [shards(): pl.pallas_call(functools.partial(kernel, n_inst, n_tp, cap), out_shape=ja...]
    dot_general x10 -> x0, matrix products: 13.9 us -> none  [the longest x2 3.91 us: local_attention(): jnp.einsum('rhd,rcd->rhc', query_heads, cached_keys, preferred_element_ty...]
    unnamed x11 -> x22, local copies, waits for them, and re-layouts: 0.03 us -> 11 us
    psum x1 -> x0, blocking collectives: 10.3 us -> none  [shards(): summed = lax.psum(partial_value, 'tp').astype(jnp.bfloat16)]
    convert_element_type x2 -> x0, other arithmetic: 1.59 us -> none  [the longest x1 1.59 us: shards(): projected = (base_sum + adapter_update).astype(jnp.bfloat16)]
    unnamed x3 -> x0, waiting for transfers between devices: 1.41 us -> none
  transfers between devices with their start and end apart: 3 -> 0, of which waited for: 2 -> 0; matrix products, arithmetic and copies ran while one was open for 12% -> 0% of each run, Pallas kernels for 0% -> 0%
where the time goes in v1:
time: 36 us; the launch traced here: 35.5 us
  Pallas kernels  24.5 us (68%)
  local copies, waits for them, and re-layouts  11 us (31%)
    pallas_call x1, Pallas kernels, shards(): pl.pallas_call(functools.partial(kernel, n_inst, n_tp, cap), out_shape=ja...  24.5 us
    unnamed x22, local copies, waits for them, and re-layouts  11 us

profile of v1, /device:TPU:0, one launch (start us, length us, event | category | flops | bytes accessed | tf_op | source)
XLA Modules:
  0.0 35.5 jit_solution(14314648785913515454)
XLA Ops:
  0.0 1.1 %copy.12.dn_hbm = bf16[4,256,64]{2,1,0:T(8,128)(2,1)S(1)} copy(bf16[4,256,64]{1,2,0:T(8,128)(2,1)} %param.18) | data formatting | bytes 262144 | tf_op args[7]
  1.1 0.0 copy-start
  1.1 1.6 %copy-done = bf16[256,4096]{1,0:T(8,128)(2,1)S(1)} copy-done((bf16[256,4096]{1,0:T(8,128)(2,1)S(1)}, bf16[256,4096]{1,0:T(8,128)(2,1)}, u32[]{:S(2)}) %copy-start) | copy-done | bytes 2097176
  2.7 0.0 copy-start.1
  2.7 1.2 %copy-done.1 = bf16[32,128,128]{2,1,0:T(8,128)(2,1)S(1)} copy-done((bf16[32,128,128]{2,1,0:T(8,128)(2,1)S(1)}, bf16[32,128,128]{2,1,0:T(8,128)(2,1)}, u32[]{:S(2)}) %copy-start.1) | copy-done | bytes 1048600
  3.9 0.0 copy-start.2
  3.9 1.2 %copy-done.2 = bf16[32,128,128]{2,1,0:T(8,128)(2,1)S(1)} copy-done((bf16[32,128,128]{2,1,0:T(8,128)(2,1)S(1)}, bf16[32,128,128]{2,1,0:T(8,128)(2,1)}, u32[]{:S(2)}) %copy-start.2) | copy-done | bytes 1048600
  5.1 0.0 copy-start.3
  5.1 1.0 %copy-done.3 = bf16[4,64,1024]{2,1,0:T(8,128)(2,1)S(1)} copy-done((bf16[4,64,1024]{2,1,0:T(8,128)(2,1)S(1)}, bf16[4,64,1024]{2,1,0:T(8,128)(2,1)}, u32[]{:S(2)}) %copy-start.3) | copy-done | bytes 524312
  6.2 0.0 copy-start.4
  6.2 0.8 %copy-done.4 = bf16[2,32,256]{2,1,0:T(8,128)(2,1)S(1)} copy-done((bf16[2,32,256]{2,1,0:T(8,128)(2,1)S(1)}, bf16[2,32,256]{2,1,0:T(8,128)(2,1)}, u32[]{:S(2)}) %copy-start.4) | copy-done | bytes 32792
  6.9 0.0 copy-start.5
  6.9 0.7 %copy-done.5 = bf16[2,32,128]{2,1,0:T(8,128)(2,1)S(1)} copy-done((bf16[2,32,128]{2,1,0:T(8,128)(2,1)S(1)}, bf16[2,32,128]{2,1,0:T(8,128)(2,1)}, u32[]{:S(2)}) %copy-start.5) | copy-done | bytes 16408
  7.6 0.0 copy-start.6
  7.6 0.7 %copy-done.6 = bf16[2,32,128]{2,1,0:T(8,128)(2,1)S(1)} copy-done((bf16[2,32,128]{2,1,0:T(8,128)(2,1)S(1)}, bf16[2,32,128]{2,1,0:T(8,128)(2,1)}, u32[]{:S(2)}) %copy-start.6) | copy-done | bytes 16408
  8.4 0.0 copy-start.7
  8.4 0.7 %copy-done.7 = s32[32]{0:T(128)S(1)} copy-done((s32[32]{0:T(128)S(1)}, s32[32]{0:T(128)}, u32[]{:S(2)}) %copy-start.7) | copy-done | bytes 152
  9.0 0.0 copy-start.8
  9.0 0.7 %copy-done.8 = s32[32,1]{0,1:T(1,128)S(1)} copy-done((s32[32,1]{0,1:T(1,128)S(1)}, s32[32,1]{0,1:T(1,128)}, u32[]{:S(2)}) %copy-start.8) | copy-done | bytes 152
  9.7 0.0 copy-start.9
  9.7 0.7 %copy-done.9 = s32[32]{0:T(128)S(1)} copy-done((s32[32]{0:T(128)S(1)}, s32[32]{0:T(128)}, u32[]{:S(2)}) %copy-start.9) | copy-done | bytes 152
  10.3 24.5 %shard_map.109 = bf16[2,32,1024]{2,1,0:T(8,128)(2,1)S(1)} custom-call(bf16[2,32,256]{2,1,0:T(8,128)(2,1)S(1)} %copy-done.4, bf16[2,32,128]{2,1,0:T(8,128)(2,1)S(1)} %copy-done.5, bf16[2,32,128]{2,1,0:T(8,128)(2,1)S(1)} %copy-done.6, s32[1,32]{1,0:T(1,128)S(1)} %bitcast.3, s32[1,32]{1,0:T(1,128)S(1)} %bitcast.4, s32[1,32]{1,0:T(1,128)S(1)} %bitcast.5, ...), custom_call_target="tpu_custom_call" | custom-call | tf_op jit(solution)/shard_map/pallas_call | solution.py:312
  34.9 0.7 %copy.14 = bf16[2,32,1024]{2,1,0:T(8,128)(2,1)} copy(bf16[2,32,1024]{2,1,0:T(8,128)(2,1)S(1)} %shard_map.109) | data formatting | bytes 262144
Async XLA Ops:
  1.1 1.6 %copy-start = (bf16[256,4096]{1,0:T(8,128)(2,1)S(1)}, bf16[256,4096]{1,0:T(8,128)(2,1)}, u32[]{:S(2)}) copy-start(bf16[256,4096]{1,0:T(8,128)(2,1)} %w_hbm.1) | copy-start | bytes 6291460
  2.7 1.2 %copy-start.1 = (bf16[32,128,128]{2,1,0:T(8,128)(2,1)S(1)}, bf16[32,128,128]{2,1,0:T(8,128)(2,1)}, u32[]{:S(2)}) copy-start(bf16[32,128,128]{2,1,0:T(8,128)(2,1)} %k_hbm.1) | copy-start | bytes 3145732
  3.9 1.2 %copy-start.2 = (bf16[32,128,128]{2,1,0:T(8,128)(2,1)S(1)}, bf16[32,128,128]{2,1,0:T(8,128)(2,1)}, u32[]{:S(2)}) copy-start(bf16[32,128,128]{2,1,0:T(8,128)(2,1)} %v_hbm.1) | copy-start | bytes 3145732
  5.1 1.0 %copy-start.3 = (bf16[4,64,1024]{2,1,0:T(8,128)(2,1)S(1)}, bf16[4,64,1024]{2,1,0:T(8,128)(2,1)}, u32[]{:S(2)}) copy-start(bf16[4,64,1024]{2,1,0:T(8,128)(2,1)} %up_hbm.1) | copy-start | bytes 1572868
  6.2 0.8 %copy-start.4 = (bf16[2,32,256]{2,1,0:T(8,128)(2,1)S(1)}, bf16[2,32,256]{2,1,0:T(8,128)(2,1)}, u32[]{:S(2)}) copy-start(bf16[2,32,256]{2,1,0:T(8,128)(2,1)} %q_ref.1) | copy-start | bytes 98308
  6.9 0.7 %copy-start.5 = (bf16[2,32,128]{2,1,0:T(8,128)(2,1)S(1)}, bf16[2,32,128]{2,1,0:T(8,128)(2,1)}, u32[]{:S(2)}) copy-start(bf16[2,32,128]{2,1,0:T(8,128)(2,1)} %kn_ref.1) | copy-start | bytes 49156
  7.6 0.7 %copy-start.6 = (bf16[2,32,128]{2,1,0:T(8,128)(2,1)S(1)}, bf16[2,32,128]{2,1,0:T(8,128)(2,1)}, u32[]{:S(2)}) copy-start(bf16[2,32,128]{2,1,0:T(8,128)(2,1)} %vn_ref.1) | copy-start | bytes 49156
  8.4 0.7 %copy-start.7 = (s32[32]{0:T(128)S(1)}, s32[32]{0:T(128)}, u32[]{:S(2)}) copy-start(s32[32]{0:T(128)} %param.16) | copy-start | bytes 388
  9.0 0.7 %copy-start.8 = (s32[32,1]{0,1:T(1,128)S(1)}, s32[32,1]{0,1:T(1,128)}, u32[]{:S(2)}) copy-start(s32[32,1]{0,1:T(1,128)} %param.20) | copy-start | bytes 388
  9.7 0.7 %copy-start.9 = (s32[32]{0:T(128)S(1)}, s32[32]{0:T(128)}, u32[]{:S(2)}) copy-start(s32[32]{0:T(128)} %param.21) | copy-start | bytes 388

commit v2 on v1

--- a/solution.py
+++ b/solution.py
@@ -42,10 +42,9 @@
 
 def kernel(
     n_inst, n_tp, cap,
-    q_ref, kn_ref, vn_ref, len_ref, host_ref, slot_ref,
-    k_hbm, v_hbm, w_hbm, dn_hbm, up_hbm,
+    host_hbm, slot_hbm, q_hbm, kn_hbm, len_hbm, k_hbm, vn_hbm, v_hbm, w_hbm, dn_hbm, up_hbm,
     out_ref,
-    k_buf, v_buf, w_buf, dn_buf, up_buf, dn_flat,
+    host_ref, slot_ref, q_ref, kn_ref, len_ref, k_buf, vn_ref, v_buf, w_buf, dn_buf, up_buf,
     meta_s, meta_r, x_s, x_r, dl_s, dl_r, rk_s, rk_r,
     b1_s, b1_r, b2_s, b2_r, own,
     in_sem, meta_ss, meta_rs, x_ss, x_rs, dl_ss, dl_rs, rk_ss, rk_rs,
@@ -59,7 +58,7 @@
     cols = rows * per_row
     pack = meta_s.shape[1]
     total = n_inst * pack
-    adapters, _, rank = dn_buf.shape
+    adapters, rank, _ = dn_buf.shape
     chunks = adapters * rank // LANES
     out_cols = up_buf.shape[2]
     n_y = n_tp // 2
@@ -80,19 +79,23 @@
             device_id=where, device_id_type=MESH,
         )
 
+    loads = []
+    for at, (src, dst) in enumerate((
+        (host_hbm, host_ref), (slot_hbm, slot_ref), (q_hbm, q_ref), (kn_hbm, kn_ref),
+        (len_hbm, len_ref), (k_hbm, k_buf), (vn_hbm, vn_ref), (v_hbm, v_buf),
+        (w_hbm, w_buf), (dn_hbm, dn_buf), (up_hbm, up_buf),
+    )):
+        load = pltpu.make_async_copy(src, dst, in_sem.at[at])
+        load.start()
+        loads.append(load)
     barrier = pltpu.get_barrier_semaphore()
     for k in range(1, n_inst):
         pl.semaphore_signal(barrier, inc=1, device_id=inst_at(k), device_id_type=MESH)
     for k in range(1, n_tp):
         pl.semaphore_signal(barrier, inc=1, device_id=tp_at(k), device_id_type=MESH)
-    loads = []
-    for at, (src, dst) in enumerate(
-        ((k_hbm, k_buf), (v_hbm, v_buf), (w_hbm, w_buf), (dn_hbm, dn_buf), (up_hbm, up_buf))
-    ):
-        load = pltpu.make_async_copy(src, dst, in_sem.at[at])
-        load.start()
-        loads.append(load)
-
+
+    loads[0].wait()
+    loads[1].wait()
     host_lane = host_ref[...].astype(F32)
     slot_lane = slot_ref[...].astype(F32)
     here = me.astype(F32)
@@ -130,6 +133,8 @@
     cj = lanes_iota((cols, cols))
     into = one_hot(cj == ((ci & (per_row - 1)) << log2(rows)) + (ci >> log2(per_row)))
     back = one_hot(ci == ((cj & (per_row - 1)) << log2(rows)) + (cj >> log2(per_row)))
+    for load in loads[2:5]:
+        load.wait()
     q_all = jnp.concatenate(
         [q_ref[s, :, h * head:(h + 1) * head] for s in range(steps) for h in range(heads)], axis=0
     )
@@ -148,7 +153,7 @@
         fresh.append(jnp.where(step_of >= s, value, -1e30))
     group = TILE // per_row
     group_of = rows_iota((TILE, slots)) >> log2(per_row)
-    loads[0].wait()
+    loads[5].wait()
     scores = []
     for g in range(rows // group):
         keys = k_buf[g * group:(g + 1) * group].reshape(group * slots, head)
@@ -169,10 +174,11 @@
         denominator += value
     weights = cached_exp / denominator
     mixed = jnp.zeros((cols, head), F32)
+    loads[6].wait()
     for s in range(steps):
         share = (fresh_exp[s] / denominator).astype(BF).astype(F32)
         mixed += share * dot(spread_bf, vn_ref[s])
-    loads[1].wait()
+    loads[7].wait()
     parts = []
     for g in range(rows // group):
         values = v_buf[g * group:(g + 1) * group].reshape(group * slots, head)
@@ -203,7 +209,7 @@
     x_r[0] = packed[:pack]
 
     feats = jnp.concatenate(features, axis=0)
-    loads[2].wait()
+    loads[8].wait()
 
     def base_part(ky, parity):
         at = (lax.rem(y + ky, n_y) * 2 + parity) * out_cols
@@ -220,12 +226,7 @@
     for ky in reversed(range(n_y)):
         own[ky] = base_part(ky, core)
 
-    loads[3].wait()
-    flat = jnp.zeros((dn_buf.shape[1], adapters * rank), F32)
-    tr, tl = rows_iota((rank, adapters * rank)), lanes_iota((rank, adapters * rank))
-    for a in range(adapters):
-        flat += dot(dn_buf[a], one_hot(tl == tr + a * rank))
-    dn_flat[...] = flat.astype(BF)
+    loads[9].wait()
     for copy in meta_copies:
         copy.wait_recv()
     slot_got = meta_r[...].reshape(total, LANES).astype(F32)
@@ -235,7 +236,9 @@
     ]
     for copy in x_copies:
         copy.wait_recv()
-    ranked = dot(x_r[...].reshape(total, width), dn_flat[...])
+    ranked = dot_t(
+        x_r[...].reshape(total, width), dn_buf[...].reshape(adapters * rank, width)
+    )
     folded = jnp.zeros((total, LANES), F32)
     for c in range(chunks):
         folded += jnp.where(masks[c], ranked[:, c * LANES:(c + 1) * LANES], 0.0)
@@ -257,7 +260,7 @@
         copy.start()
         b2_copies.append(copy)
 
-    loads[4].wait()
+    loads[10].wait()
     for k, copy in enumerate(rk_copies, 1):
         copy.wait_recv()
         folded += rk_r[k].astype(F32)
@@ -306,21 +309,21 @@
     total = n_inst * pack
     n_y = n_tp // 2
     lines = steps * rows
+    operands = (
+        host.reshape(1, rows), slot.reshape(1, rows), queries, incoming_keys,
+        cache_length_rows.reshape(1, rows), stored_keys, incoming_values, stored_values,
+        output_matrix, jnp.swapaxes(adapter_down_weight, 1, 2), adapter_up_weight,
+    )
     vmem = pl.BlockSpec(memory_space=pltpu.VMEM)
-    far = pl.BlockSpec(memory_space=pl.ANY)
+    far = pl.BlockSpec(memory_space=pltpu.HBM)
     sem = pltpu.SemaphoreType.DMA
     return pl.pallas_call(
         functools.partial(kernel, n_inst, n_tp, cap),
         out_shape=jax.ShapeDtypeStruct((steps, rows, out_cols), BF),
-        in_specs=[vmem] * 6 + [far] * 5,
+        in_specs=[far] * len(operands),
         out_specs=vmem,
         scratch_shapes=[
-            pltpu.VMEM(stored_keys.shape, BF),
-            pltpu.VMEM(stored_values.shape, BF),
-            pltpu.VMEM(output_matrix.shape, BF),
-            pltpu.VMEM(adapter_down_weight.shape, BF),
-            pltpu.VMEM(adapter_up_weight.shape, BF),
-            pltpu.VMEM((width, adapters * rank), BF),
+            *[pltpu.VMEM(operand.shape, operand.dtype) for operand in operands],
             pltpu.VMEM((n_inst, pack, LANES), BF),
             pltpu.VMEM((n_inst, pack, LANES), BF),
             pltpu.VMEM((n_inst, pack, width), BF),
@@ -334,7 +337,7 @@
             pltpu.VMEM((n_y, lines, out_cols), BF),
             pltpu.VMEM((n_y, lines, out_cols), BF),
             pltpu.VMEM((n_y, lines, out_cols), F32),
-            sem((5,)),
+            sem((len(operands),)),
             sem((n_inst,)), sem((n_inst,)),
             sem((n_inst,)), sem((n_inst,)),
             sem((n_inst,)), sem((n_inst,)),
@@ -343,13 +346,9 @@
             sem((n_y,)), sem((n_y,)),
         ],
         compiler_params=pltpu.CompilerParams(
-            collective_id=0, has_side_effects=True, vmem_limit_bytes=48 * 1024 * 1024
+            collective_id=0, has_side_effects=True, vmem_limit_bytes=60 * 1024 * 1024
         ),
-    )(
-        queries, incoming_keys, incoming_values,
-        cache_length_rows.reshape(1, rows), host.reshape(1, rows), slot.reshape(1, rows),
-        stored_keys, stored_values, output_matrix, adapter_down_weight, adapter_up_weight,
-    )
+    )(*operands)
 
 
 def solution(mesh):

time: 36 us -> 27.2 us (0.76)
  local copies, waits for them, and re-layouts: 11 us -> 1.57 us
  Pallas kernels: 24.5 us -> 25.5 us
    unnamed x22 -> x1, local copies, waits for them, and re-layouts: 11 us -> 1.57 us
    pallas_call x1, Pallas kernels: 24.5 us -> 25.5 us  [shards(): pl.pallas_call(functools.partial(kernel, n_inst, n_tp, cap), out_shape=ja...]
where the time goes in v2:
time: 27.2 us; the launch traced here: 27 us
  Pallas kernels  25.5 us (94%)
  local copies, waits for them, and re-layouts  1.57 us (6%)
    pallas_call x1, Pallas kernels, shards(): pl.pallas_call(functools.partial(kernel, n_inst, n_tp, cap), out_shape=ja...  25.5 us
    unnamed x1, local copies, waits for them, and re-layouts  1.57 us

profile of v2, /device:TPU:0, one launch (start us, length us, event | category | flops | bytes accessed | tf_op | source)
XLA Modules:
  0.0 27.0 jit_solution(11597999642795911256)
XLA Ops:
  0.0 25.5 %shard_map.109 = bf16[2,32,1024]{2,1,0:T(8,128)(2,1)} custom-call(s32[1,32]{1,0:T(1,128)} %bitcast.5, s32[1,32]{1,0:T(1,128)} %bitcast.6, bf16[2,32,256]{2,1,0:T(8,128)(2,1)} %q_hbm.1, bf16[2,32,128]{2,1,0:T(8,128)(2,1)} %kn_hbm.1, s32[1,32]{1,0:T(1,128)} %bitcast.7, bf16[32,128,128]{2,1,0:T(8,128)(2,1)} %k_hbm.1, bf16[2,32,128]{2,1,0:T(8,128)(2,1)} %vn_hbm.1, ...), custom_call_target="tpu_custom_call" | custom-call | tf_op jit(solution)/shard_map/pallas_call | solution.py:320
  25.5 1.6 %copy.13 = bf16[2,32,1024]{2,1,0:T(8,128)(2,1)} copy(bf16[2,32,1024]{2,1,0:T(8,128)(2,1)} %shard_map.109) | data formatting | bytes 262144

commit v3 on v2

--- a/solution.py
+++ b/solution.py
@@ -45,9 +45,9 @@
     host_hbm, slot_hbm, q_hbm, kn_hbm, len_hbm, k_hbm, vn_hbm, v_hbm, w_hbm, dn_hbm, up_hbm,
     out_ref,
     host_ref, slot_ref, q_ref, kn_ref, len_ref, k_buf, vn_ref, v_buf, w_buf, dn_buf, up_buf,
-    meta_s, meta_r, x_s, x_r, dl_s, dl_r, rk_s, rk_r,
+    x_s, x_r, dl_s, dl_r, rk_s, rk_r,
     b1_s, b1_r, b2_s, b2_r, own,
-    in_sem, meta_ss, meta_rs, x_ss, x_rs, dl_ss, dl_rs, rk_ss, rk_rs,
+    in_sem, x_ss, x_rs, dl_ss, dl_rs, rk_ss, rk_rs,
     b1_ss, b1_rs, b2_ss, b2_rs,
 ):
     steps, rows, width = q_ref.shape
@@ -56,7 +56,7 @@
     slots = k_buf.shape[1]
     per_row = steps * heads
     cols = rows * per_row
-    pack = meta_s.shape[1]
+    pack = x_s.shape[1]
     total = n_inst * pack
     adapters, rank, _ = dn_buf.shape
     chunks = adapters * rank // LANES
@@ -79,6 +79,7 @@
             device_id=where, device_id_type=MESH,
         )
 
+    far_first = sorted(range(1, n_inst), key=lambda k: -min(k, n_inst - k))
     loads = []
     for at, (src, dst) in enumerate((
         (host_hbm, host_ref), (slot_hbm, slot_ref), (q_hbm, q_ref), (kn_hbm, kn_ref),
@@ -119,15 +120,8 @@
     for chosen in packs:
         slot_packed += jnp.sum(jnp.where(chosen, slot_lane, 0.0), axis=1, keepdims=True)
     slot_packed = jnp.broadcast_to(slot_packed, (total, LANES)).astype(BF)
-    meta_s[...] = slot_packed.reshape(n_inst, pack, LANES)
-    meta_r[0] = slot_packed[:pack]
-
-    pl.semaphore_wait(barrier, n_inst - 1 + n_tp - 1)
-    meta_copies = []
-    for k in range(1, n_inst):
-        copy = remote(meta_s.at[k], meta_r.at[k], meta_ss.at[k], meta_rs.at[k], inst_at(k))
-        copy.start()
-        meta_copies.append(copy)
+    x_s[:, :, width:] = slot_packed.reshape(n_inst, pack, LANES)
+    x_r[0, :, width:] = slot_packed[:pack]
 
     ci = rows_iota((cols, cols))
     cj = lanes_iota((cols, cols))
@@ -200,13 +194,14 @@
     for s in range(1, steps):
         packed += dot(one_hot(packs[s]), features[s])
     packed = packed.astype(BF)
-    x_s[...] = packed.reshape(n_inst, pack, width)
+    x_s[:, :, :width] = packed.reshape(n_inst, pack, width)
+    pl.semaphore_wait(barrier, n_inst - 1 + n_tp - 1)
     x_copies = []
-    for k in range(1, n_inst):
+    for k in far_first:
         copy = remote(x_s.at[k], x_r.at[k], x_ss.at[k], x_rs.at[k], inst_at(k))
         copy.start()
         x_copies.append(copy)
-    x_r[0] = packed[:pack]
+    x_r[0, :, :width] = packed[:pack]
 
     feats = jnp.concatenate(features, axis=0)
     loads[8].wait()
@@ -223,21 +218,16 @@
         )
         copy.start()
         b1_copies[ky] = copy
-    for ky in reversed(range(n_y)):
-        own[ky] = base_part(ky, core)
-
     loads[9].wait()
-    for copy in meta_copies:
+    for copy in x_copies:
         copy.wait_recv()
-    slot_got = meta_r[...].reshape(total, LANES).astype(F32)
+    slot_got = x_r[:, :, width:].reshape(total, LANES).astype(F32)
     lane = lanes_iota((total, LANES))
     masks = [
         slot_got == ((lane + c * LANES) >> log2(rank)).astype(F32) for c in range(chunks)
     ]
-    for copy in x_copies:
-        copy.wait_recv()
     ranked = dot_t(
-        x_r[...].reshape(total, width), dn_buf[...].reshape(adapters * rank, width)
+        x_r[:, :, :width].reshape(total, width), dn_buf[...].reshape(adapters * rank, width)
     )
     folded = jnp.zeros((total, LANES), F32)
     for c in range(chunks):
@@ -249,6 +239,8 @@
         copy.start()
         rk_copies.append(copy)
 
+    for ky in reversed(range(n_y)):
+        own[ky] = base_part(ky, core)
     b2_copies = []
     for ky in range(1, n_y):
         b1_copies[ky].wait_recv()
@@ -270,7 +262,7 @@
     delta = dot(wide, up_buf[...].reshape(adapters * rank, out_cols)).astype(BF)
     dl_s[...] = delta.reshape(n_inst, pack, out_cols)
     dl_copies = []
-    for k in range(1, n_inst):
+    for k in far_first:
         copy = remote(dl_s.at[k], dl_r.at[k], dl_ss.at[k], dl_rs.at[k], inst_at(-k))
         copy.start()
         dl_copies.append(copy)
@@ -290,7 +282,7 @@
     result = own[0] + dot(unpack, dl_r[...].reshape(total, out_cols))
     out_ref[...] = result.astype(BF).reshape(steps, rows, out_cols)
 
-    for copy in meta_copies + x_copies + rk_copies + b2_copies + dl_copies:
+    for copy in x_copies + rk_copies + b2_copies + dl_copies:
         copy.wait_send()
     for ky in range(n_y):
         b1_copies[ky].wait_send()
@@ -324,10 +316,8 @@
         out_specs=vmem,
         scratch_shapes=[
             *[pltpu.VMEM(operand.shape, operand.dtype) for operand in operands],
-            pltpu.VMEM((n_inst, pack, LANES), BF),
-            pltpu.VMEM((n_inst, pack, LANES), BF),
-            pltpu.VMEM((n_inst, pack, width), BF),
-            pltpu.VMEM((n_inst, pack, width), BF),
+            pltpu.VMEM((n_inst, pack, width + LANES), BF),
+            pltpu.VMEM((n_inst, pack, width + LANES), BF),
             pltpu.VMEM((n_inst, pack, out_cols), BF),
             pltpu.VMEM((n_inst, pack, out_cols), BF),
             pltpu.VMEM((total, LANES), BF),
@@ -338,7 +328,6 @@
             pltpu.VMEM((n_y, lines, out_cols), BF),
             pltpu.VMEM((n_y, lines, out_cols), F32),
             sem((len(operands),)),
-            sem((n_inst,)), sem((n_inst,)),
             sem((n_inst,)), sem((n_inst,)),
             sem((n_inst,)), sem((n_inst,)),
             sem((n_tp,)), sem((n_tp,)),

time: 27.2 us -> 25.4 us (0.934)
  Pallas kernels: 25.5 us -> 23.6 us
    pallas_call x1, Pallas kernels: 25.5 us -> 23.6 us  [shards(): pl.pallas_call(functools.partial(kernel, n_inst, n_tp, cap), out_shape=ja...]
where the time goes in v3:
time: 25.4 us; the launch traced here: 25.2 us
  Pallas kernels  23.6 us (93%)
  local copies, waits for them, and re-layouts  1.57 us (6%)
    pallas_call x1, Pallas kernels, shards(): pl.pallas_call(functools.partial(kernel, n_inst, n_tp, cap), out_shape=ja...  23.6 us
    unnamed x1, local copies, waits for them, and re-layouts  1.57 us

profile of v3, /device:TPU:0, one launch (start us, length us, event | category | flops | bytes accessed | tf_op | source)
XLA Modules:
  0.0 25.2 jit_solution(18254373179499918090)
XLA Ops:
  0.0 23.6 %shard_map.109 = bf16[2,32,1024]{2,1,0:T(8,128)(2,1)} custom-call(s32[1,32]{1,0:T(1,128)} %bitcast.5, s32[1,32]{1,0:T(1,128)} %bitcast.6, bf16[2,32,256]{2,1,0:T(8,128)(2,1)} %q_hbm.1, bf16[2,32,128]{2,1,0:T(8,128)(2,1)} %kn_hbm.1, s32[1,32]{1,0:T(1,128)} %bitcast.7, bf16[32,128,128]{2,1,0:T(8,128)(2,1)} %k_hbm.1, bf16[2,32,128]{2,1,0:T(8,128)(2,1)} %vn_hbm.1, ...), custom_call_target="tpu_custom_call" | custom-call | tf_op jit(solution)/shard_map/pallas_call | solution.py:312
  23.6 1.6 %copy.13 = bf16[2,32,1024]{2,1,0:T(8,128)(2,1)} copy(bf16[2,32,1024]{2,1,0:T(8,128)(2,1)} %shard_map.109) | data formatting | bytes 262144

commit v4 on v3

--- a/solution.py
+++ b/solution.py
@@ -59,6 +59,7 @@
     pack = x_s.shape[1]
     total = n_inst * pack
     adapters, rank, _ = dn_buf.shape
+    assert 2 * rank == LANES
     chunks = adapters * rank // LANES
     out_cols = up_buf.shape[2]
     n_y = n_tp // 2
@@ -87,7 +88,8 @@
         (w_hbm, w_buf), (dn_hbm, dn_buf), (up_hbm, up_buf),
     )):
         load = pltpu.make_async_copy(src, dst, in_sem.at[at])
-        load.start()
+        if at < 8:
+            load.start()
         loads.append(load)
     barrier = pltpu.get_barrier_semaphore()
     for k in range(1, n_inst):
@@ -148,6 +150,8 @@
     group = TILE // per_row
     group_of = rows_iota((TILE, slots)) >> log2(per_row)
     loads[5].wait()
+    for load in loads[8:]:
+        load.start()
     scores = []
     for g in range(rows // group):
         keys = k_buf[g * group:(g + 1) * group].reshape(group * slots, head)
@@ -232,7 +236,11 @@
     folded = jnp.zeros((total, LANES), F32)
     for c in range(chunks):
         folded += jnp.where(masks[c], ranked[:, c * LANES:(c + 1) * LANES], 0.0)
-    rk_s[...] = folded.astype(BF)
+    half = total // 2
+    left = lanes_iota((half, LANES)) < rank
+    both = folded + pltpu.roll(folded, LANES - rank, 1)
+    paired = jnp.where(left, both[:half], both[half:])
+    rk_s[...] = paired.astype(BF)
     rk_copies = []
     for k in range(1, n_tp):
         copy = remote(rk_s, rk_r.at[k], rk_ss.at[k], rk_rs.at[k], tp_at(k))
@@ -255,7 +263,11 @@
     loads[10].wait()
     for k, copy in enumerate(rk_copies, 1):
         copy.wait_recv()
-        folded += rk_r[k].astype(F32)
+        paired += rk_r[k].astype(F32)
+    turned = pltpu.roll(paired, LANES - rank, 1)
+    folded = jnp.concatenate(
+        [jnp.where(left, paired, turned), jnp.where(left, turned, paired)], axis=0
+    )
     wide = jnp.concatenate(
         [jnp.where(masks[c], folded, 0.0) for c in range(chunks)], axis=1
     ).astype(BF)
@@ -311,7 +323,7 @@
     sem = pltpu.SemaphoreType.DMA
     return pl.pallas_call(
         functools.partial(kernel, n_inst, n_tp, cap),
-        out_shape=jax.ShapeDtypeStruct((steps, rows, out_cols), BF),
+        out_shape=pltpu.VMEM((steps, rows, out_cols), BF),
         in_specs=[far] * len(operands),
         out_specs=vmem,
         scratch_shapes=[
@@ -320,8 +332,8 @@
             pltpu.VMEM((n_inst, pack, width + LANES), BF),
             pltpu.VMEM((n_inst, pack, out_cols), BF),
             pltpu.VMEM((n_inst, pack, out_cols), BF),
-            pltpu.VMEM((total, LANES), BF),
-            pltpu.VMEM((n_tp, total, LANES), BF),
+            pltpu.VMEM((total // 2, LANES), BF),
+            pltpu.VMEM((n_tp, total // 2, LANES), BF),
             pltpu.VMEM((n_y, lines, out_cols), BF),
             pltpu.VMEM((n_y, lines, out_cols), BF),
             pltpu.VMEM((n_y, lines, out_cols), BF),

time: 25.4 us -> 23.6 us (0.929)
  local copies, waits for them, and re-layouts: 1.57 us -> 0.66 us
  Pallas kernels: 23.6 us -> 22.8 us
    unnamed x1, local copies, waits for them, and re-layouts: 1.57 us -> 0.66 us
    pallas_call x1, Pallas kernels: 23.6 us -> 22.8 us  [shards(): pl.pallas_call(functools.partial(kernel, n_inst, n_tp, cap), out_shape=pl...]
where the time goes in v4:
time: 23.6 us; the launch traced here: 23.5 us
  Pallas kernels  22.8 us (97%)
  local copies, waits for them, and re-layouts  0.66 us (3%)
    pallas_call x1, Pallas kernels, shards(): pl.pallas_call(functools.partial(kernel, n_inst, n_tp, cap), out_shape=pl...  22.8 us
    unnamed x1, local copies, waits for them, and re-layouts  0.66 us

profile of v4, /device:TPU:0, one launch (start us, length us, event | category | flops | bytes accessed | tf_op | source)
XLA Modules:
  0.0 23.5 jit_solution(11772087868477956875)
XLA Ops:
  0.0 22.8 %shard_map.109 = bf16[2,32,1024]{2,1,0:T(8,128)(2,1)S(1)} custom-call(s32[1,32]{1,0:T(1,128)} %bitcast.5, s32[1,32]{1,0:T(1,128)} %bitcast.6, bf16[2,32,256]{2,1,0:T(8,128)(2,1)} %q_hbm.1, bf16[2,32,128]{2,1,0:T(8,128)(2,1)} %kn_hbm.1, s32[1,32]{1,0:T(1,128)} %bitcast.7, bf16[32,128,128]{2,1,0:T(8,128)(2,1)} %k_hbm.1, bf16[2,32,128]{2,1,0:T(8,128)(2,1)} %vn_hbm.1, ...), custom_call_target="tpu_custom_call" | custom-call | tf_op jit(solution)/shard_map/pallas_call | solution.py:324
  22.8 0.7 %copy.13 = bf16[2,32,1024]{2,1,0:T(8,128)(2,1)} copy(bf16[2,32,1024]{2,1,0:T(8,128)(2,1)S(1)} %shard_map.109) | data formatting | bytes 262144

commit v5 on v4

--- a/solution.py
+++ b/solution.py
@@ -13,6 +13,7 @@
 F32 = jnp.float32
 TILE = 16
 LANES = 128
+PIECES = 4
 
 
 def log2(n):
@@ -88,9 +89,19 @@
         (w_hbm, w_buf), (dn_hbm, dn_buf), (up_hbm, up_buf),
     )):
         load = pltpu.make_async_copy(src, dst, in_sem.at[at])
-        if at < 8:
+        if at < 8 and at not in (5, 7):
             load.start()
         loads.append(load)
+    piece = rows // PIECES
+    key_loads, value_loads = [], []
+    for src, dst, kept, first in (
+        (k_hbm, k_buf, key_loads, 11), (v_hbm, v_buf, value_loads, 11 + PIECES)
+    ):
+        for c in range(PIECES):
+            at = pl.ds(c * piece, piece)
+            load = pltpu.make_async_copy(src.at[at], dst.at[at], in_sem.at[first + c])
+            load.start()
+            kept.append(load)
     barrier = pltpu.get_barrier_semaphore()
     for k in range(1, n_inst):
         pl.semaphore_signal(barrier, inc=1, device_id=inst_at(k), device_id_type=MESH)
@@ -149,11 +160,13 @@
         fresh.append(jnp.where(step_of >= s, value, -1e30))
     group = TILE // per_row
     group_of = rows_iota((TILE, slots)) >> log2(per_row)
-    loads[5].wait()
+    per_piece = piece // group
     for load in loads[8:]:
         load.start()
     scores = []
     for g in range(rows // group):
+        if g % per_piece == 0:
+            key_loads[g // per_piece].wait()
         keys = k_buf[g * group:(g + 1) * group].reshape(group * slots, head)
         raw = dot_t(q_bf[g * TILE:(g + 1) * TILE], keys)
         picked = raw[:, :slots]
@@ -176,9 +189,10 @@
     for s in range(steps):
         share = (fresh_exp[s] / denominator).astype(BF).astype(F32)
         mixed += share * dot(spread_bf, vn_ref[s])
-    loads[7].wait()
     parts = []
     for g in range(rows // group):
+        if g % per_piece == 0:
+            value_loads[g // per_piece].wait()
         values = v_buf[g * group:(g + 1) * group].reshape(group * slots, head)
         own_w = weights[g * TILE:(g + 1) * TILE]
         blocked = jnp.concatenate(
@@ -339,7 +353,7 @@
             pltpu.VMEM((n_y, lines, out_cols), BF),
             pltpu.VMEM((n_y, lines, out_cols), BF),
             pltpu.VMEM((n_y, lines, out_cols), F32),
-            sem((len(operands),)),
+            sem((len(operands) + 2 * PIECES,)),
             sem((n_inst,)), sem((n_inst,)),
             sem((n_inst,)), sem((n_inst,)),
             sem((n_tp,)), sem((n_tp,)),

time: 23.6 us -> 23.9 us (1.013)
    pallas_call x1, Pallas kernels: 22.8 us -> 23 us  [shards(): pl.pallas_call(functools.partial(kernel, n_inst, n_tp, cap), out_shape=pl...]
where the time goes in v5:
time: 23.9 us; the launch traced here: 23.7 us
  Pallas kernels  23 us (96%)
  local copies, waits for them, and re-layouts  0.66 us (3%)
    pallas_call x1, Pallas kernels, shards(): pl.pallas_call(functools.partial(kernel, n_inst, n_tp, cap), out_shape=pl...  23 us
    unnamed x1, local copies, waits for them, and re-layouts  0.66 us

profile of v5, /device:TPU:0, one launch (start us, length us, event | category | flops | bytes accessed | tf_op | source)
XLA Modules:
  0.0 23.7 jit_solution(17292684236291822013)
XLA Ops:
  0.0 23.0 %shard_map.109 = bf16[2,32,1024]{2,1,0:T(8,128)(2,1)S(1)} custom-call(s32[1,32]{1,0:T(1,128)} %bitcast.5, s32[1,32]{1,0:T(1,128)} %bitcast.6, bf16[2,32,256]{2,1,0:T(8,128)(2,1)} %q_hbm.1, bf16[2,32,128]{2,1,0:T(8,128)(2,1)} %kn_hbm.1, s32[1,32]{1,0:T(1,128)} %bitcast.7, bf16[32,128,128]{2,1,0:T(8,128)(2,1)} %k_hbm.1, bf16[2,32,128]{2,1,0:T(8,128)(2,1)} %vn_hbm.1, ...), custom_call_target="tpu_custom_call" | custom-call | tf_op jit(solution)/shard_map/pallas_call | solution.py:338
  23.1 0.7 %copy.13 = bf16[2,32,1024]{2,1,0:T(8,128)(2,1)} copy(bf16[2,32,1024]{2,1,0:T(8,128)(2,1)S(1)} %shard_map.109) | data formatting | bytes 262144
